TPU v7x, 32 devices: a whole 2x2x4 slice. The times are simulated.
32 devices in a mesh: parts: 2 (over y), rows: 4 (over z), cols: 2 (over x), sub: 2 (over core).
Axes of the slice: x: 2, y: 2, z: 4, core: 2. Of those that a mesh axis runs over, the one named last changes fastest.
Arguments:
- right_side: float32 [128, 8192], P(('parts', 'cols'), ('rows', 'sub')), parts along dimension 0, may hold values from -6 to 6
- start_field: float32 [128, 8192], P(('parts', 'cols'), ('rows', 'sub')), parts along dimension 0, may hold values from -4 to 4
- fine_tiles: bfloat16 [128, 3, 128, 128], P(('parts', 'rows', 'sub')), parts along dimension 0, as said below
- fine_links: int32 [128, 3], P(('parts', 'rows', 'sub')), parts along dimension 0, may hold values from 0 to 9, as said below
- fine_groups: int32 [16384], P(('parts', 'rows', 'sub')), parts along dimension 0, may hold values from 0 to 511, as said below
- mid_tiles: bfloat16 [8, 3, 128, 128], P('parts'), parts along dimension 0, as said below
- mid_links: int32 [8, 3], P('parts'), parts along dimension 0, may hold values from 0 to 3, as said below
- mid_groups: int32 [1024], P('parts'), parts along dimension 0, may hold values from 0 to 255
- last_inverse: float32 [512, 256], P('parts'), parts along dimension 0
Outputs:
- solution: float32 [128, 8192], P(('parts', 'cols'), ('rows', 'sub')), parts along dimension 0
There are 2 independent parts, one for each index of `parts`. A program takes and returns all parts, laid end to end along the dimension named above; each array names one. Nothing has to cross between parts.
Inputs may be any that keep to these rules, and one draw needn't show every extreme that they name: `fine_links`: entry 0 of fine block row g is g % 8 + 1, the row's own block; entry 1 of every row with g % 8 = 0 is 0 and entry 2 of every row with g % 8 = 7 is 9. `fine_groups`: fine cell c belongs to a middle cell from w * (c // 1024) to w * (c // 1024) + w - 1, where w = 64. `mid_links`: entry 0 of middle block row g is g. `fine_tiles`: the diagonal of each tile [g, 0] exceeds the sum of magnitudes of the rest of its row by 0.1 or more; all other entries are at most 0. `mid_tiles`: as for fine_tiles, with every entry 16 times larger.
All inputs are finite; a program needn't handle non-finite values.
Results may differ from a plain program's by a relative error of at most 0.0003.
The roundings to bfloat16 on the way count: a program that leaves them out, or rounds other values in their place, can miss the bound.
Values may be sent and summed in bfloat16 or wider, within the bound.
A program may use at most 64 MiB of HBM per device.

v0:
```python
import jax
import jax.numpy as jnp
from jax import lax
from jax.sharding import PartitionSpec as P

damping = 0.6


def extended(x, sides, width):
    for axis, dim in sides:
        size, length = (lax.axis_size(axis), x.shape[dim])
        up = [(i, (i + 1) % size) for i in range(size - 1)]
        down = [(j, i) for i, j in up]
        last = lax.slice_in_dim(x, length - width, length, axis=dim)
        first = lax.slice_in_dim(x, 0, width, axis=dim)
        before = lax.ppermute(last, axis, up)
        after = lax.ppermute(first, axis, down)
        x = jnp.concatenate([before, x, after], axis=dim)
    return x


def fine_apply(field, fine_tiles, fine_links):
    rounded = field.astype(jnp.bfloat16)
    padded = extended(rounded, ((("rows", "sub"), 1),), fine_tiles.shape[2])
    blocks = padded.reshape(field.shape[0], -1, fine_tiles.shape[2])
    picked = blocks[:, fine_links]
    result = jnp.einsum("snkc,nkrc->snr", picked, fine_tiles, preferred_element_type=jnp.float32)
    return result.reshape(field.shape)


def tile_apply(whole, tiles, links, out_shape):
    blocks = whole.reshape(whole.shape[0], -1, tiles.shape[2])
    picked = blocks[:, links]
    result = jnp.einsum("snkc,nkrc->snr", picked, tiles, preferred_element_type=jnp.float32)
    return result.reshape(out_shape)


def shards(
    right_side,
    start_field,
    fine_tiles,
    fine_links,
    fine_groups,
    mid_tiles,
    mid_links,
    mid_groups,
    last_inverse,
):
    tile = fine_tiles.shape[2]
    mid_cells = mid_tiles.shape[0] * tile
    last_cells = last_inverse.shape[0]
    window = mid_cells // lax.axis_size(("rows", "sub"))
    offset = lax.axis_index(("rows", "sub")) * window
    fine_diag = jnp.diagonal(fine_tiles[:, 0].astype(jnp.float32), axis1=1, axis2=2).reshape(-1)
    mid_diag = jnp.diagonal(mid_tiles[:, 0].astype(jnp.float32), axis1=1, axis2=2).reshape(-1)
    field = start_field
    for sweep in range(2):
        field = (
            field + damping * (right_side - fine_apply(field, fine_tiles, fine_links)) / fine_diag
        )
    fine_resid = right_side - fine_apply(field, fine_tiles, fine_links)
    fine_pick = (
        (fine_groups - offset)[:, None] == jnp.arange(window, dtype=jnp.int32)[None, :]
    ).astype(jnp.float32)
    partial_side = jnp.dot(fine_resid, fine_pick, precision=lax.Precision.HIGHEST)
    mid_side = lax.all_gather(partial_side, ("rows", "sub"), axis=1, tiled=True)

    def full_apply(values):
        return tile_apply(values.astype(jnp.bfloat16), mid_tiles, mid_links, values.shape)

    coarse_pick = (mid_groups[:, None] == jnp.arange(last_cells, dtype=jnp.int32)[None, :]).astype(
        jnp.float32
    )
    mid_field = damping * mid_side / mid_diag
    mid_field = mid_field + damping * (mid_side - full_apply(mid_field)) / mid_diag
    mid_resid = mid_side - full_apply(mid_field)
    last_part = jnp.dot(mid_resid, coarse_pick, precision=lax.Precision.HIGHEST)
    last_fix = jnp.dot(last_part, last_inverse.T, precision=lax.Precision.HIGHEST)
    mid_field = mid_field + jnp.dot(last_fix, coarse_pick.T, precision=lax.Precision.HIGHEST)
    for middle_sweep in range(2):
        mid_field = mid_field + damping * (mid_side - full_apply(mid_field)) / mid_diag
    mid_window = lax.dynamic_slice_in_dim(mid_field, offset, window, 1)
    field = field + jnp.dot(mid_window, fine_pick.T, precision=lax.Precision.HIGHEST)
    for sweep in range(2):
        field = (
            field + damping * (right_side - fine_apply(field, fine_tiles, fine_links)) / fine_diag
        )
    return field


def solution(mesh):
    in_specs = (
        P(("parts", "cols"), ("rows", "sub")),
        P(("parts", "cols"), ("rows", "sub")),
        P(("parts", "rows", "sub"), None, None, None),
        P(("parts", "rows", "sub"), None),
        P(("parts", "rows", "sub")),
        P("parts", None, None, None),
        P("parts", None),
        P("parts"),
        P("parts", None),
    )
    out_specs = P(("parts", "cols"), ("rows", "sub"))
    return jax.shard_map(shards, mesh=mesh, in_specs=in_specs, out_specs=out_specs, check_vma=False)
```

profile of v0, /device:TPU:1, one launch (start us, length us, event | category | flops | bytes accessed | tf_op | source)
XLA Modules:
  0.0 86.6 jit_solution(14967751623868476084)
XLA Ops:
  0.0 1.0 %convert_element_type.41 = bf16[32,1024]{1,0:T(8,128)(2,1)S(1)} convert(f32[32,1024]{1,0:T(8,128)} %param.10) | non-fusion elementwise | flops 32768 | bytes 196608 | tf_op jit(solution)/shard_map/convert_element_type | solution.py:23
  1.0 4.6 %collective-permute-start = (bf16[32,128]{1,0:T(8,128)(2,1)S(1)}, bf16[32,128]{1,0:T(8,128)(2,1)S(1)}, u32[]{:S(2)}, u32[]{:S(2)}) collective-permute-start(bf16[32,128]{1,0:T(8,128)(2,1)S(1)} %get-tuple-element.19), channel_id=1, source_target_pairs={{0,1},{1,4},{4,5},{5,8},{8,9},{9,12},{12,13},{2,3},{3,6},{6,7},{7,... | collective-permute-start | bytes 24584 | tf_op jit(solution)/shard_map/ppermute | solution.py:16
  5.6 1.9 %collective-permute-start.1 = (bf16[32,128]{1,0:T(8,128)(2,1)S(1)}, bf16[32,128]{1,0:T(8,128)(2,1)S(1)}, u32[]{:S(2)}, u32[]{:S(2)}) collective-permute-start(bf16[32,128]{1,0:T(8,128)(2,1)S(1)} %get-tuple-element.20), channel_id=1, source_target_pairs={{1,0},{4,1},{5,4},{8,5},{9,8},{12,9},{13,12},{3,2},{6,3},{7,6},{10... | collective-permute-start | bytes 24584 | tf_op jit(solution)/shard_map/ppermute | solution.py:17
  7.5 0.7 compare_select_fusion.1
  8.2 0.1 copy.50
  8.3 0.1 reshape.84
  8.4 1.0 %slice.38 = bf16[8,1,128,128]{3,2,1,0:T(8,128)(2,1)S(1)} slice(bf16[8,3,128,128]{3,2,1,0:T(8,128)(2,1)} %param.11), slice={[0:8], [0:1], [0:128], [0:128]} | slice | bytes 524288 | tf_op jit(solution)/shard_map/slice | solution.py:54
  9.3 0.0 slice-start
  9.4 3.2 %copy.53 = bf16[8,1,128,128]{0,3,2,1:T(8,128)(2,1)} copy(bf16[8,1,128,128]{3,2,1,0:T(8,128)(2,1)S(1)} %slice.38) | data formatting | bytes 524288 | tf_op jit(solution)/shard_map/slice | solution.py:54
  12.6 6.5 %bitcast_convert_fusion.1 = f32[8,128,128]{0,2,1:T(8,128)} fusion(bf16[8,1,128,128]{0,3,2,1:T(8,128)(2,1)} %copy.53), kind=kLoop, calls=%fused_computation.12 | loop fusion | flops 131072 | bytes 786432 | tf_op jit(solution)/shard_map/convert_element_type | solution.py:54
  19.1 0.0 copy-start.4
  19.1 3.3 %copy.60 = bf16[4,1,128,128]{0,3,2,1:T(8,128)(2,1)} copy(bf16[4,1,128,128]{3,2,1,0:T(8,128)(2,1)S(1)} %slice-done) | data formatting | bytes 262144 | tf_op jit(solution)/shard_map/slice | solution.py:55
  22.4 6.5 %bitcast_convert_fusion = f32[4,128,128]{0,2,1:T(8,128)} fusion(bf16[4,1,128,128]{0,3,2,1:T(8,128)(2,1)} %copy.60), kind=kLoop, calls=%fused_computation.11 | loop fusion | flops 65536 | bytes 393216 | tf_op jit(solution)/shard_map/convert_element_type | solution.py:55
  29.0 1.8 %gather_fusion.1 = f32[128,8]{1,0:T(8,128)S(1)} fusion(f32[8,128,128]{0,2,1:T(8,128)} %bitcast_convert_fusion.1, s32[128]{0:T(128)S(1)} %or_bitcast_fusion), kind=kCustom, calls=%fused_computation.1 | custom fusion | bytes 9216 | tf_op jit(solution)/shard_map/jit(diagonal)/gather | solution.py:54
  30.8 0.0 collective-permute-done
  30.8 0.0 collective-permute-done.1
  30.8 0.6 gather_fusion
  31.4 0.4 convolution_bitcast_fusion.4
  31.8 0.0 copy-done.4
  31.9 3.6 %collective-permute-start.2 = (bf16[32,128]{1,0:T(8,128)(2,1)S(1)}, bf16[32,128]{1,0:T(8,128)(2,1)S(1)}, u32[]{:S(2)}, u32[]{:S(2)}) collective-permute-start(bf16[32,128]{1,0:T(8,128)(2,1)S(1)} %get-tuple-element.17), channel_id=1, source_target_pairs={{0,1},{1,4},{4,5},{5,8},{8,9},{9,12},{12,13},{2,3},{3,6},{6,7},{7,... | collective-permute-start | bytes 24584 | tf_op jit(solution)/shard_map/ppermute | solution.py:16
  35.5 1.9 %collective-permute-start.3 = (bf16[32,128]{1,0:T(8,128)(2,1)S(1)}, bf16[32,128]{1,0:T(8,128)(2,1)S(1)}, u32[]{:S(2)}, u32[]{:S(2)}) collective-permute-start(bf16[32,128]{1,0:T(8,128)(2,1)S(1)} %get-tuple-element.18), channel_id=1, source_target_pairs={{1,0},{4,1},{5,4},{8,5},{9,8},{12,9},{13,12},{3,2},{6,3},{7,6},{10... | collective-permute-start | bytes 24584 | tf_op jit(solution)/shard_map/ppermute | solution.py:17
  37.5 0.1 reshape.120
  37.6 0.0 collective-permute-done.2
  37.6 2.9 %collective-permute-done.3 = bf16[32,128]{1,0:T(8,128)(2,1)S(1)} collective-permute-done((bf16[32,128]{1,0:T(8,128)(2,1)S(1)}, bf16[32,128]{1,0:T(8,128)(2,1)S(1)}, u32[]{:S(2)}, u32[]{:S(2)}) %collective-permute-start.3) | collective-permute-done | bytes 8224 | tf_op jit(solution)/shard_map/ppermute | solution.py:17
  40.5 0.6 gather_fusion.2
  41.1 0.4 convolution_bitcast_fusion.3
  41.5 0.1 fusion.40
  41.6 1.9 %collective-permute-start.4 = (bf16[32,128]{1,0:T(8,128)(2,1)S(1)}, bf16[32,128]{1,0:T(8,128)(2,1)S(1)}, u32[]{:S(2)}, u32[]{:S(2)}) collective-permute-start(bf16[32,128]{1,0:T(8,128)(2,1)S(1)} %get-tuple-element.15), channel_id=1, source_target_pairs={{0,1},{1,4},{4,5},{5,8},{8,9},{9,12},{12,13},{2,3},{3,6},{6,7},{7,... | collective-permute-start | bytes 24584 | tf_op jit(solution)/shard_map/ppermute | solution.py:16
  43.5 2.4 %collective-permute-start.5 = (bf16[32,128]{1,0:T(8,128)(2,1)S(1)}, bf16[32,128]{1,0:T(8,128)(2,1)S(1)}, u32[]{:S(2)}, u32[]{:S(2)}) collective-permute-start(bf16[32,128]{1,0:T(8,128)(2,1)S(1)} %get-tuple-element.16), channel_id=1, source_target_pairs={{1,0},{4,1},{5,4},{8,5},{9,8},{12,9},{13,12},{3,2},{6,3},{7,6},{10... | collective-permute-start | bytes 24584 | tf_op jit(solution)/shard_map/ppermute | solution.py:17
  45.9 1.8 %gather_fusion.4 = f32[128,4]{1,0:T(8,128)S(1)} fusion(f32[4,128,128]{0,2,1:T(8,128)} %bitcast_convert_fusion, s32[128]{0:T(128)S(1)} %or_bitcast_fusion), kind=kCustom, calls=%fused_computation.4 | custom fusion | bytes 5120 | tf_op jit(solution)/shard_map/jit(diagonal)/gather | solution.py:55
  47.7 0.1 copy.61
  47.7 0.1 dynamic-slice
  47.8 0.7 collective-permute-done.5
  48.5 0.6 gather_fusion.3
  49.1 0.4 convolution_bitcast_fusion.2
  49.5 0.4 convolution_bitcast_fusion.9
  49.9 13.6 %all-gather = f32[8,64,32]{1,2,0:T(8,128)S(1)} all-gather(f32[1,64,32]{1,2,0:T(8,128)S(1)} %convolution_bitcast_fusion.9), channel_id=1, replica_groups=mesh['parts'=2,'rows'=4,'cols'=2,'sub'=2] {'rows','sub'}, dimensions={0}, use_global_device_ids=true | all-gather | bytes 73728 | tf_op jit(solution)/shard_map/all_gather | solution.py:66
  63.5 0.1 copy.59
  63.6 0.1 reshape.185
  63.7 0.6 gather_fusion.5
  64.3 0.2 convolution_bitcast_fusion.8
  64.6 0.6 gather_fusion.6
  65.1 0.2 convolution_bitcast_fusion.7
  65.4 0.4 fusion
  65.7 0.3 fusion.48
  66.1 0.4 convolution_add_fusion.1
  66.5 0.6 gather_fusion.7
  67.1 0.2 convolution_bitcast_fusion.6
  67.4 0.6 gather_fusion.8
  68.0 0.2 convolution_bitcast_fusion.5
  68.2 0.5 fusion.47
  68.8 3.1 %collective-permute-start.6 = (bf16[32,128]{1,0:T(8,128)(2,1)S(1)}, bf16[32,128]{1,0:T(8,128)(2,1)S(1)}, u32[]{:S(2)}, u32[]{:S(2)}) collective-permute-start(bf16[32,128]{1,0:T(8,128)(2,1)S(1)} %get-tuple-element.13), channel_id=1, source_target_pairs={{0,1},{1,4},{4,5},{5,8},{8,9},{9,12},{12,13},{2,3},{3,6},{6,7},{7,... | collective-permute-start | bytes 24584 | tf_op jit(solution)/shard_map/ppermute | solution.py:16
  71.9 1.9 %collective-permute-start.7 = (bf16[32,128]{1,0:T(8,128)(2,1)S(1)}, bf16[32,128]{1,0:T(8,128)(2,1)S(1)}, u32[]{:S(2)}, u32[]{:S(2)}) collective-permute-start(bf16[32,128]{1,0:T(8,128)(2,1)S(1)} %get-tuple-element.14), channel_id=1, source_target_pairs={{1,0},{4,1},{5,4},{8,5},{9,8},{12,9},{13,12},{3,2},{6,3},{7,6},{10... | collective-permute-start | bytes 24584 | tf_op jit(solution)/shard_map/ppermute | solution.py:17
  73.9 0.0 collective-permute-done.6
  73.9 3.0 %collective-permute-done.7 = bf16[32,128]{1,0:T(8,128)(2,1)S(1)} collective-permute-done((bf16[32,128]{1,0:T(8,128)(2,1)S(1)}, bf16[32,128]{1,0:T(8,128)(2,1)S(1)}, u32[]{:S(2)}, u32[]{:S(2)}) %collective-permute-start.7) | collective-permute-done | bytes 8224 | tf_op jit(solution)/shard_map/ppermute | solution.py:17
  76.9 0.6 gather_fusion.9
  77.5 0.4 convolution_bitcast_fusion.1
  77.9 0.1 fusion.37
  78.0 1.9 %collective-permute-start.8 = (bf16[32,128]{1,0:T(8,128)(2,1)S(1)}, bf16[32,128]{1,0:T(8,128)(2,1)S(1)}, u32[]{:S(2)}, u32[]{:S(2)}) collective-permute-start(bf16[32,128]{1,0:T(8,128)(2,1)S(1)} %get-tuple-element.11), channel_id=1, source_target_pairs={{0,1},{1,4},{4,5},{5,8},{8,9},{9,12},{12,13},{2,3},{3,6},{6,7},{7,... | collective-permute-start | bytes 24584 | tf_op jit(solution)/shard_map/ppermute | solution.py:16
  79.9 2.4 %collective-permute-start.9 = (bf16[32,128]{1,0:T(8,128)(2,1)S(1)}, bf16[32,128]{1,0:T(8,128)(2,1)S(1)}, u32[]{:S(2)}, u32[]{:S(2)}) collective-permute-start(bf16[32,128]{1,0:T(8,128)(2,1)S(1)} %get-tuple-element.12), channel_id=1, source_target_pairs={{1,0},{4,1},{5,4},{8,5},{9,8},{12,9},{13,12},{3,2},{6,3},{7,6},{10... | collective-permute-start | bytes 24584 | tf_op jit(solution)/shard_map/ppermute | solution.py:17
  82.3 2.6 %collective-permute-done.9 = bf16[32,128]{1,0:T(8,128)(2,1)S(1)} collective-permute-done((bf16[32,128]{1,0:T(8,128)(2,1)S(1)}, bf16[32,128]{1,0:T(8,128)(2,1)S(1)}, u32[]{:S(2)}, u32[]{:S(2)}) %collective-permute-start.9) | collective-permute-done | bytes 8224 | tf_op jit(solution)/shard_map/ppermute | solution.py:17
  84.9 0.6 gather_fusion.10
  85.5 0.4 convolution_bitcast_fusion
  85.9 0.7 fusion.7
  (41 shorter events, 0.4 us)
Async XLA Ops:
  0.0 65.7 %copy-start = (f32[256,256]{1,0:T(8,128)S(1)}, f32[256,256]{1,0:T(8,128)}, u32[]{:S(2)}) copy-start(f32[256,256]{1,0:T(8,128)} %param.17) | copy-start | bytes 786436
  1.0 29.8 %collective-permute-start = (bf16[32,128]{1,0:T(8,128)(2,1)S(1)}, bf16[32,128]{1,0:T(8,128)(2,1)S(1)}, u32[]{:S(2)}, u32[]{:S(2)}) collective-permute-start(bf16[32,128]{1,0:T(8,128)(2,1)S(1)} %get-tuple-element.19), channel_id=1, source_target_pairs={{0,1},{1,4},{4,5},{5,8},{8,9},{9,12},{12,13},{2,3},{3,6},{6,7},{7,... | collective-permute-start | bytes 24584 | tf_op jit(solution)/shard_map/ppermute | solution.py:16
  5.6 25.2 %collective-permute-start.1 = (bf16[32,128]{1,0:T(8,128)(2,1)S(1)}, bf16[32,128]{1,0:T(8,128)(2,1)S(1)}, u32[]{:S(2)}, u32[]{:S(2)}) collective-permute-start(bf16[32,128]{1,0:T(8,128)(2,1)S(1)} %get-tuple-element.20), channel_id=1, source_target_pairs={{1,0},{4,1},{5,4},{8,5},{9,8},{12,9},{13,12},{3,2},{6,3},{7,6},{10... | collective-permute-start | bytes 24584 | tf_op jit(solution)/shard_map/ppermute | solution.py:17
  9.3 9.8 %slice-start = ((bf16[4,3,128,128]{3,2,1,0:T(8,128)(2,1)}), bf16[4,1,128,128]{3,2,1,0:T(8,128)(2,1)S(1)}, s32[]{:S(2)}) async-start(bf16[4,3,128,128]{3,2,1,0:T(8,128)(2,1)} %param.14), calls=%async_computation | async-start | bytes 262144 | tf_op jit(solution)/shard_map/slice | solution.py:55
  19.1 9.8 %copy-start.5 = (s32[1024]{0:T(1024)S(1)}, s32[1024]{0:T(1024)}, u32[]{:S(2)}) copy-start(s32[1024]{0:T(1024)} %param.13) | copy-start | bytes 12292
  19.1 12.3 %copy-start.1 = (bf16[8,3,128,128]{3,2,1,0:T(8,128)(2,1)S(1)}, bf16[8,3,128,128]{3,2,1,0:T(8,128)(2,1)}, u32[]{:S(2)}) copy-start(bf16[8,3,128,128]{3,2,1,0:T(8,128)(2,1)} %param.11) | copy-start | bytes 2359300
  19.1 12.7 %copy-start.3 = (f32[32,1024]{1,0:T(8,128)S(1)}, f32[32,1024]{1,0:T(8,128)}, u32[]{:S(2)}) copy-start(f32[32,1024]{1,0:T(8,128)} %param.9) | copy-start | bytes 393220
  19.1 12.7 %copy-start.4 = (f32[32,1024]{1,0:T(8,128)S(1)}, f32[32,1024]{1,0:T(8,128)}, u32[]{:S(2)}) copy-start(f32[32,1024]{1,0:T(8,128)} %param.10) | copy-start | bytes 393220
  22.4 15.0 %copy-start.6 = (s32[4,3]{1,0:T(4,128)S(1)}, s32[4,3]{1,0:T(4,128)}, u32[]{:S(2)}) copy-start(s32[4,3]{1,0:T(4,128)} %param.15) | copy-start | bytes 148
  22.4 41.8 %copy-start.2 = (bf16[4,3,128,128]{3,2,1,0:T(8,128)(2,1)S(1)}, bf16[4,3,128,128]{3,2,1,0:T(8,128)(2,1)}, u32[]{:S(2)}) copy-start(bf16[4,3,128,128]{3,2,1,0:T(8,128)(2,1)} %param.14) | copy-start | bytes 1179652
  22.4 43.0 %copy-start.7 = (s32[512]{0:T(512)S(1)}, s32[512]{0:T(512)}, u32[]{:S(2)}) copy-start(s32[512]{0:T(512)} %param.16) | copy-start | bytes 6148
  31.9 5.7 %collective-permute-start.2 = (bf16[32,128]{1,0:T(8,128)(2,1)S(1)}, bf16[32,128]{1,0:T(8,128)(2,1)S(1)}, u32[]{:S(2)}, u32[]{:S(2)}) collective-permute-start(bf16[32,128]{1,0:T(8,128)(2,1)S(1)} %get-tuple-element.17), channel_id=1, source_target_pairs={{0,1},{1,4},{4,5},{5,8},{8,9},{9,12},{12,13},{2,3},{3,6},{6,7},{7,... | collective-permute-start | bytes 24584 | tf_op jit(solution)/shard_map/ppermute | solution.py:16
  35.5 5.0 %collective-permute-start.3 = (bf16[32,128]{1,0:T(8,128)(2,1)S(1)}, bf16[32,128]{1,0:T(8,128)(2,1)S(1)}, u32[]{:S(2)}, u32[]{:S(2)}) collective-permute-start(bf16[32,128]{1,0:T(8,128)(2,1)S(1)} %get-tuple-element.18), channel_id=1, source_target_pairs={{1,0},{4,1},{5,4},{8,5},{9,8},{12,9},{13,12},{3,2},{6,3},{7,6},{10... | collective-permute-start | bytes 24584 | tf_op jit(solution)/shard_map/ppermute | solution.py:17
  41.6 6.3 %collective-permute-start.4 = (bf16[32,128]{1,0:T(8,128)(2,1)S(1)}, bf16[32,128]{1,0:T(8,128)(2,1)S(1)}, u32[]{:S(2)}, u32[]{:S(2)}) collective-permute-start(bf16[32,128]{1,0:T(8,128)(2,1)S(1)} %get-tuple-element.15), channel_id=1, source_target_pairs={{0,1},{1,4},{4,5},{5,8},{8,9},{9,12},{12,13},{2,3},{3,6},{6,7},{7,... | collective-permute-start | bytes 24584 | tf_op jit(solution)/shard_map/ppermute | solution.py:16
  43.5 5.0 %collective-permute-start.5 = (bf16[32,128]{1,0:T(8,128)(2,1)S(1)}, bf16[32,128]{1,0:T(8,128)(2,1)S(1)}, u32[]{:S(2)}, u32[]{:S(2)}) collective-permute-start(bf16[32,128]{1,0:T(8,128)(2,1)S(1)} %get-tuple-element.16), channel_id=1, source_target_pairs={{1,0},{4,1},{5,4},{8,5},{9,8},{12,9},{13,12},{3,2},{6,3},{7,6},{10... | collective-permute-start | bytes 24584 | tf_op jit(solution)/shard_map/ppermute | solution.py:17
  68.8 5.1 %collective-permute-start.6 = (bf16[32,128]{1,0:T(8,128)(2,1)S(1)}, bf16[32,128]{1,0:T(8,128)(2,1)S(1)}, u32[]{:S(2)}, u32[]{:S(2)}) collective-permute-start(bf16[32,128]{1,0:T(8,128)(2,1)S(1)} %get-tuple-element.13), channel_id=1, source_target_pairs={{0,1},{1,4},{4,5},{5,8},{8,9},{9,12},{12,13},{2,3},{3,6},{6,7},{7,... | collective-permute-start | bytes 24584 | tf_op jit(solution)/shard_map/ppermute | solution.py:16
  71.9 5.0 %collective-permute-start.7 = (bf16[32,128]{1,0:T(8,128)(2,1)S(1)}, bf16[32,128]{1,0:T(8,128)(2,1)S(1)}, u32[]{:S(2)}, u32[]{:S(2)}) collective-permute-start(bf16[32,128]{1,0:T(8,128)(2,1)S(1)} %get-tuple-element.14), channel_id=1, source_target_pairs={{1,0},{4,1},{5,4},{8,5},{9,8},{12,9},{13,12},{3,2},{6,3},{7,6},{10... | collective-permute-start | bytes 24584 | tf_op jit(solution)/shard_map/ppermute | solution.py:17
  78.0 4.3 %collective-permute-start.8 = (bf16[32,128]{1,0:T(8,128)(2,1)S(1)}, bf16[32,128]{1,0:T(8,128)(2,1)S(1)}, u32[]{:S(2)}, u32[]{:S(2)}) collective-permute-start(bf16[32,128]{1,0:T(8,128)(2,1)S(1)} %get-tuple-element.11), channel_id=1, source_target_pairs={{0,1},{1,4},{4,5},{5,8},{8,9},{9,12},{12,13},{2,3},{3,6},{6,7},{7,... | collective-permute-start | bytes 24584 | tf_op jit(solution)/shard_map/ppermute | solution.py:16
  79.9 5.0 %collective-permute-start.9 = (bf16[32,128]{1,0:T(8,128)(2,1)S(1)}, bf16[32,128]{1,0:T(8,128)(2,1)S(1)}, u32[]{:S(2)}, u32[]{:S(2)}) collective-permute-start(bf16[32,128]{1,0:T(8,128)(2,1)S(1)} %get-tuple-element.12), channel_id=1, source_target_pairs={{1,0},{4,1},{5,4},{8,5},{9,8},{12,9},{13,12},{3,2},{6,3},{7,6},{10... | collective-permute-start | bytes 24584 | tf_op jit(solution)/shard_map/ppermute | solution.py:17
where the time goes:
time: 87.1 us; the launch traced here: 86.6 us
  starting transfers between devices  25.8 us (30%)
  local copies, waits for them, and re-layouts  16.9 us (19%)
  other arithmetic  15.8 us (18%)
  blocking collectives  13.6 us (16%)
  waiting for transfers between devices  9.21 us (11%)
  matrix products  4.82 us (6%)
    ppermute x5, starting transfers between devices, extended(): before = lax.ppermute(last, axis, up)  15.3 us
    all_gather x1, blocking collectives, shards(): mid_side = lax.all_gather(partial_side, ('rows', 'sub'), axis=1, tiled=True)  13.6 us
    ppermute x5, starting transfers between devices, extended(): after = lax.ppermute(first, axis, down)  10.5 us
    ppermute x5, waiting for transfers between devices, extended(): after = lax.ppermute(first, axis, down)  9.2 us
    convert_element_type x1, other arithmetic, shards(): fine_tiles[:, 0].astype(jnp.float32)  6.54 us
    convert_element_type x1, other arithmetic, shards(): mid_tiles[:, 0].astype(jnp.float32)  6.53 us
    slice x2, local copies, waits for them, and re-layouts, shards(): fine_tiles[:, 0].astype(jnp.float32)  4.18 us
    slice x3, local copies, waits for them, and re-layouts, shards(): mid_tiles[:, 0].astype(jnp.float32)  3.28 us
  transfers between devices with their start and end apart: 10, of which 4 were waited for; matrix products, arithmetic and copies ran while one was open for 29% of the time, Pallas kernels for 0%

commit v1 on v0

v1 whole, which is shorter than its diff:
```python
import functools

import jax
import jax.numpy as jnp
from jax import lax
from jax.experimental import pallas as pl
from jax.experimental.pallas import tpu as pltpu
from jax.sharding import PartitionSpec as P

damping = 0.6
MESH = pl.DeviceIdType.MESH
F32 = jnp.float32
BF16 = jnp.bfloat16


def dot_nt(a, b):
    return lax.dot_general(a, b, (((1,), (1,)), ((), ())), preferred_element_type=F32)


def dot_nn(a, b):
    return lax.dot_general(a, b, (((1,), (0,)), ((), ())), preferred_element_type=F32)


def pieces(x, count):
    out = []
    for _ in range(count):
        high = x.astype(BF16)
        out.append(high)
        x = x - high.astype(F32)
    return jnp.concatenate(out, axis=0)


def unstack(y, count):
    rows = y.shape[0] // count
    total = y[(count - 1) * rows :]
    for i in range(count - 2, -1, -1):
        total = y[i * rows : (i + 1) * rows] + total
    return total


def one_hot_t(groups, base, rows):
    ids = lax.broadcasted_iota(jnp.int32, (rows, groups.shape[1]), 0) + base
    return jnp.where(ids == groups, 1.0, 0.0).astype(BF16)


def scale_of(tile):
    size = tile.shape[0]
    row = lax.broadcasted_iota(jnp.int32, (size, size), 0)
    col = lax.broadcasted_iota(jnp.int32, (size, size), 1)
    return damping / jnp.sum(jnp.where(row == col, tile.astype(F32), 0.0), axis=0, keepdims=True)


def kernel(
    n,
    sub,
    links,
    mid_links,
    b_any,
    u_any,
    t_any,
    grp_any,
    mt_any,
    mg_any,
    li_any,
    out_ref,
    b_v,
    u_v,
    t_v,
    grp_v,
    mt_v,
    mg_v,
    li_v,
    xb0,
    xb1,
    xb2,
    xb3,
    xb4,
    halo_f,
    ends_f,
    grp_h,
    slabs,
    pt,
    ct,
    e_hi,
    e_lo,
    mb,
    mid_v,
    load_sem,
    halo_send,
    halo_recv,
    all_send,
    all_recv,
):
    blocks, tile = t_v.shape[0], t_v.shape[2]
    mid_blocks = mt_v.shape[0]
    last = li_v.shape[0]
    per = n // mid_blocks
    me = lax.axis_index("rows") * sub + lax.axis_index("sub")
    has_left = me > 0
    has_right = me < n - 1

    def place(j):
        return {"rows": lax.div(j, sub), "sub": lax.rem(j, sub)}

    loads = [
        pltpu.make_async_copy(src, dst, load_sem.at[i])
        for i, (src, dst) in enumerate(
            (
                (u_any, u_v),
                (grp_any, grp_v),
                (t_any, t_v),
                (b_any, b_v),
                (mg_any, mg_v),
                (li_any, li_v),
                (mt_any, mt_v),
            )
        )
    ]
    for load in loads:
        load.start()

    barrier = pltpu.get_barrier_semaphore()
    for off in range(1, n):
        pl.semaphore_signal(
            barrier, inc=1, device_id=place(lax.rem(me + off, n)), device_id_type=MESH
        )

    left = jnp.maximum(me - 1, 0)
    right = jnp.minimum(me + 1, n - 1)

    def to_left(i, src, dst):
        return pltpu.make_async_remote_copy(
            src_ref=src,
            dst_ref=dst,
            send_sem=halo_send.at[i, 0],
            recv_sem=halo_recv.at[i, 1],
            device_id=place(left),
            device_id_type=MESH,
        )

    def to_right(i, src, dst):
        return pltpu.make_async_remote_copy(
            src_ref=src,
            dst_ref=dst,
            send_sem=halo_send.at[i, 1],
            recv_sem=halo_recv.at[i, 0],
            device_id=place(right),
            device_id_type=MESH,
        )

    def pair(i, first, final, before, after):
        return to_left(i, first, after), to_right(i, final, before)

    def ends(i, xb):
        return pair(i, xb.at[1], xb.at[blocks], xb.at[0], xb.at[blocks + 1])

    swaps = [
        ends(0, xb0),
        ends(1, xb1),
        pair(2, ends_f.at[0], ends_f.at[1], halo_f.at[0], halo_f.at[1]),
        ends(3, xb4),
        pair(4, grp_v, grp_v, grp_h.at[0], grp_h.at[1]),
    ]

    def send(i):
        @pl.when(has_left)
        def _():
            swaps[i][0].start()

        @pl.when(has_right)
        def _():
            swaps[i][1].start()

    def recv(i):
        @pl.when(has_left)
        def _():
            swaps[i][1].wait_recv()

        @pl.when(has_right)
        def _():
            swaps[i][0].wait_recv()

    def sent(i):
        @pl.when(has_left)
        def _():
            swaps[i][0].wait_send()

        @pl.when(has_right)
        def _():
            swaps[i][1].wait_send()

    zero_b = jnp.zeros(xb0.shape[1:], BF16)
    zero_f = jnp.zeros(halo_f.shape[1:], F32)

    @pl.when(me == 0)
    def _():
        for xb in (xb0, xb1, xb4):
            xb[0] = zero_b
        halo_f[0] = zero_f
        grp_h[0] = jnp.zeros(grp_h.shape[1:], jnp.int32)

    @pl.when(me == n - 1)
    def _():
        for xb in (xb0, xb1, xb4):
            xb[blocks + 1] = zero_b
        halo_f[1] = zero_f
        grp_h[1] = jnp.zeros(grp_h.shape[1:], jnp.int32)

    order = [0, blocks - 1] + list(range(1, blocks - 1))
    cells = [slice(g * tile, (g + 1) * tile) for g in range(blocks)]

    loads[0].wait()
    for g in order:
        xb0[g + 1] = u_v[:, cells[g]].astype(BF16)
    loads[1].wait()
    pl.semaphore_wait(barrier, n - 1)
    send(0)
    send(4)

    def own(xb):
        return [dot_nt(xb[g + 1], t_v[g, 0]) for g in range(blocks)]

    def rest(xb, g):
        picked = jnp.concatenate([xb[links[g, 1]], xb[links[g, 2]]], axis=1)
        return dot_nt(picked, jnp.concatenate([t_v[g, 1], t_v[g, 2]], axis=1))

    loads[2].wait()
    loads[3].wait()
    acc = own(xb0)
    scale = [scale_of(t_v[g, 0]) for g in range(blocks)]
    base = lax.div(me, per) * tile
    for g in range(blocks):
        pt[:, cells[g]] = one_hot_t(grp_v[g : g + 1], base, tile)

    recv(0)
    for g in order:
        new = u_v[:, cells[g]] + (b_v[:, cells[g]] - (acc[g] + rest(xb0, g))) * scale[g]
        u_v[:, cells[g]] = new
        xb1[g + 1] = new.astype(BF16)
        if g == blocks - 1:
            send(1)
    acc = own(xb1)

    for i in (4, 5, 6):
        loads[i].wait()
    flipped = li_v[...].T
    flipped_hi = flipped.astype(BF16)
    flipped_lo = (flipped - flipped_hi.astype(F32)).astype(BF16)
    for m in range(mid_blocks):
        hot = one_hot_t(mg_v[m : m + 1], 0, last)
        ct[m] = hot
        e_hi[m] = dot_nn(flipped_hi, hot).astype(BF16)
        e_lo[m] = dot_nn(flipped_lo, hot).astype(BF16)

    recv(1)
    for g in order:
        new = u_v[:, cells[g]] + (b_v[:, cells[g]] - (acc[g] + rest(xb1, g))) * scale[g]
        u_v[:, cells[g]] = new
        xb2[g + 1] = new.astype(BF16)
        if g == 0:
            ends_f[0] = new
        if g == blocks - 1:
            ends_f[1] = new
            send(2)
    acc = own(xb2)
    mid_scale = [scale_of(mt_v[m, 0]) for m in range(mid_blocks)]

    recv(2)
    xb2[0] = halo_f[0].astype(BF16)
    xb2[blocks + 1] = halo_f[1].astype(BF16)
    resid = jnp.concatenate(
        [pieces(b_v[:, cells[g]] - (acc[g] + rest(xb2, g)), 3) for g in range(blocks)], axis=1
    )
    slabs[me] = unstack(dot_nt(resid, pt[...]), 3)
    gathers = []
    for off in range(n - 1, 0, -1):
        copy = pltpu.make_async_remote_copy(
            src_ref=slabs.at[me],
            dst_ref=slabs.at[me],
            send_sem=all_send.at[off - 1],
            recv_sem=all_recv.at[off - 1],
            device_id=place(lax.rem(me + off, n)),
            device_id_type=MESH,
        )
        copy.start()
        gathers.append(copy)
    recv(4)
    hot_left = one_hot_t(grp_h[0, blocks - 1 : blocks], lax.div(left, per) * tile, tile)
    hot_right = one_hot_t(grp_h[1, 0:1], lax.div(right, per) * tile, tile)
    for copy in gathers:
        copy.wait_recv()

    side = []
    for m in range(mid_blocks):
        total = slabs[m * per]
        for i in range(1, per):
            total = total + slabs[m * per + i]
        side.append(total)

    def mid_apply(values):
        for m in range(mid_blocks):
            mb[m] = values[m].astype(BF16)
        out = []
        for m in range(mid_blocks):
            picked = jnp.concatenate(
                [mb[m], mb[mid_links[m, 1]], mb[mid_links[m, 2]]], axis=1
            )
            out.append(
                dot_nt(picked, jnp.concatenate([mt_v[m, 0], mt_v[m, 1], mt_v[m, 2]], axis=1))
            )
        return out

    def mid_sweep(values):
        return [
            v + (s - a) * d for v, s, a, d in zip(values, side, mid_apply(values), mid_scale)
        ]

    mid = [s * d for s, d in zip(side, mid_scale)]
    mid = mid_sweep(mid)
    mid_resid = [s - a for s, a in zip(side, mid_apply(mid))]
    last_side = dot_nt(pieces(mid_resid[0], 2), ct[0])
    for m in range(1, mid_blocks):
        last_side = last_side + dot_nt(pieces(mid_resid[m], 2), ct[m])
    both = pieces(unstack(last_side, 2), 2)
    high = both[: both.shape[0] // 2]
    mid = [
        mid[m] + (unstack(dot_nn(both, e_hi[m]), 2) + dot_nn(high, e_lo[m]))
        for m in range(mid_blocks)
    ]
    mid = mid_sweep(mid)
    mid = mid_sweep(mid)
    for m in range(mid_blocks):
        mid_v[m] = mid[m]

    def lift(device, hot):
        return unstack(dot_nn(pieces(mid_v[lax.div(device, per)], 3), hot), 3)

    add = lift(me, pt[...])
    before = halo_f[0] + lift(left, hot_left)
    after = halo_f[1] + lift(right, hot_right)
    xb3[0] = jnp.where(has_left, before, 0.0).astype(BF16)
    xb3[blocks + 1] = jnp.where(has_right, after, 0.0).astype(BF16)
    for g in range(blocks):
        new = u_v[:, cells[g]] + add[:, cells[g]]
        u_v[:, cells[g]] = new
        xb3[g + 1] = new.astype(BF16)

    acc = own(xb3)
    for g in order:
        new = u_v[:, cells[g]] + (b_v[:, cells[g]] - (acc[g] + rest(xb3, g))) * scale[g]
        u_v[:, cells[g]] = new
        xb4[g + 1] = new.astype(BF16)
        if g == blocks - 1:
            send(3)
    acc = own(xb4)

    recv(3)
    for g in range(blocks):
        out_ref[:, cells[g]] = (
            u_v[:, cells[g]] + (b_v[:, cells[g]] - (acc[g] + rest(xb4, g))) * scale[g]
        )
    for i in range(len(swaps)):
        sent(i)
    for copy in gathers:
        copy.wait_send()


def shards(
    right_side,
    start_field,
    fine_tiles,
    fine_links,
    fine_groups,
    mid_tiles,
    mid_links,
    mid_groups,
    last_inverse,
):
    sub = lax.axis_size("sub")
    n = lax.axis_size("rows") * sub
    blocks, _, tile, _ = fine_tiles.shape
    mid_blocks = mid_tiles.shape[0]
    rows = right_side.shape[0]
    last = last_inverse.shape[0]
    anywhere = pl.BlockSpec(memory_space=pl.ANY)
    scalars = pl.BlockSpec(memory_space=pltpu.SMEM)
    groups = fine_groups.reshape(blocks, tile)
    mid_groups = mid_groups.reshape(mid_blocks, tile)
    large = [right_side, start_field, fine_tiles, groups, mid_tiles, mid_groups, last_inverse]
    held = pltpu.VMEM((blocks + 2, rows, tile), BF16)
    return pl.pallas_call(
        functools.partial(kernel, n, sub),
        out_shape=jax.ShapeDtypeStruct(right_side.shape, F32),
        in_specs=[scalars] * 2 + [anywhere] * len(large),
        out_specs=pl.BlockSpec(memory_space=pltpu.VMEM),
        scratch_shapes=[pltpu.VMEM(x.shape, x.dtype) for x in large]
        + [held] * 5
        + [
            pltpu.VMEM((2, rows, tile), F32),
            pltpu.VMEM((2, rows, tile), F32),
            pltpu.VMEM((2, blocks, tile), jnp.int32),
            pltpu.VMEM((n, rows, tile), F32),
            pltpu.VMEM((tile, blocks * tile), BF16),
            pltpu.VMEM((mid_blocks, last, tile), BF16),
            pltpu.VMEM((mid_blocks, last, tile), BF16),
            pltpu.VMEM((mid_blocks, last, tile), BF16),
            pltpu.VMEM((mid_blocks, rows, tile), BF16),
            pltpu.VMEM((mid_blocks, rows, tile), F32),
            pltpu.SemaphoreType.DMA((len(large),)),
            pltpu.SemaphoreType.DMA((5, 2)),
            pltpu.SemaphoreType.DMA((5, 2)),
            pltpu.SemaphoreType.DMA((n - 1,)),
            pltpu.SemaphoreType.DMA((n - 1,)),
        ],
        compiler_params=pltpu.CompilerParams(
            collective_id=0, has_side_effects=True, vmem_limit_bytes=48 * 1024 * 1024
        ),
    )(fine_links, mid_links, *large)


def solution(mesh):
    in_specs = (
        P(("parts", "cols"), ("rows", "sub")),
        P(("parts", "cols"), ("rows", "sub")),
        P(("parts", "rows", "sub"), None, None, None),
        P(("parts", "rows", "sub"), None),
        P(("parts", "rows", "sub")),
        P("parts", None, None, None),
        P("parts", None),
        P("parts"),
        P("parts", None),
    )
    out_specs = P(("parts", "cols"), ("rows", "sub"))
    return jax.shard_map(shards, mesh=mesh, in_specs=in_specs, out_specs=out_specs, check_vma=False)
```

time: 87.1 us -> 28.4 us (0.33)
  starting transfers between devices: 25.8 us -> 0 us
  Pallas kernels: 0 us -> 21.7 us
  other arithmetic: 15.8 us -> 0 us
  blocking collectives: 13.6 us -> 0 us
  local copies, waits for them, and re-layouts: 16.9 us -> 6.34 us
  waiting for transfers between devices: 9.21 us -> 0 us
  matrix products: 4.82 us -> 0 us
    ppermute x10 -> x0, starting transfers between devices: 25.8 us -> none  [the longest x5 15.3 us: extended(): before = lax.ppermute(last, axis, up)]
    pallas_call x0 -> x1, Pallas kernels: none -> 21.7 us  [shards(): pl.pallas_call(functools.partial(kernel, n, sub), out_shape=jax.ShapeDtyp...]
    convert_element_type x6 -> x0, other arithmetic: 14.2 us -> none  [the longest x1 6.54 us: shards(): fine_tiles[:, 0].astype(jnp.float32)]
    all_gather x1 -> x0, blocking collectives: 13.6 us -> none  [shards(): mid_side = lax.all_gather(partial_side, ('rows', 'sub'), axis=1, tiled=True)]
    ppermute x10 -> x0, waiting for transfers between devices: 9.21 us -> none  [the longest x5 9.2 us: extended(): after = lax.ppermute(first, axis, down)]
    gather x13 -> x0, local copies, waits for them, and re-layouts: 8.82 us -> none  [the longest x5 2.92 us: fine_apply(): picked = blocks[:, fine_links]]
    slice x10 -> x0, local copies, waits for them, and re-layouts: 7.49 us -> none  [the longest x2 4.18 us: shards(): fine_tiles[:, 0].astype(jnp.float32)]
    unnamed x17 -> x18, local copies, waits for them, and re-layouts: 0.14 us -> 6.34 us
  transfers between devices with their start and end apart: 10 -> 0, of which waited for: 4 -> 0; matrix products, arithmetic and copies ran while one was open for 29% -> 0% of each run, Pallas kernels for 0% -> 0%
where the time goes in v1:
time: 28.4 us; the launch traced here: 28.1 us
  Pallas kernels  21.7 us (76%)
  local copies, waits for them, and re-layouts  6.34 us (22%)
    pallas_call x1, Pallas kernels, shards(): pl.pallas_call(functools.partial(kernel, n, sub), out_shape=jax.ShapeDtyp...  21.7 us
    unnamed x18, local copies, waits for them, and re-layouts  6.34 us

profile of v1, /device:TPU:1, one launch (start us, length us, event | category | flops | bytes accessed | tf_op | source)
XLA Modules:
  0.0 28.1 jit_solution(11953960188858124851)
XLA Ops:
  0.0 0.0 copy-start.7
  0.0 0.0 copy-start.5
  0.0 0.0 copy-start.6
  0.0 0.8 %copy.10.links = s32[8,3]{1,0:T(8,128)S(1)} copy(s32[8,3]{0,1:T(4,128)} %param.12) | data formatting | bytes 192 | tf_op args[3]
  0.8 0.0 copy-done.7
  0.8 0.0 copy-done.5
  0.8 0.0 copy-done.6
  0.8 0.0 copy-start
  0.8 1.1 %copy-done = bf16[8,3,128,128]{3,2,1,0:T(8,128)(2,1)S(1)} copy-done((bf16[8,3,128,128]{3,2,1,0:T(8,128)(2,1)S(1)}, bf16[8,3,128,128]{3,2,1,0:T(8,128)(2,1)}, u32[]{:S(2)}) %copy-start) | copy-done | bytes 786456
  1.9 0.0 copy-start.1
  1.9 1.0 %copy-done.1 = bf16[4,3,128,128]{3,2,1,0:T(8,128)(2,1)S(1)} copy-done((bf16[4,3,128,128]{3,2,1,0:T(8,128)(2,1)S(1)}, bf16[4,3,128,128]{3,2,1,0:T(8,128)(2,1)}, u32[]{:S(2)}) %copy-start.1) | copy-done | bytes 393240
  2.9 0.0 copy-start.2
  2.9 0.9 %copy-done.2 = f32[256,256]{1,0:T(8,128)S(1)} copy-done((f32[256,256]{1,0:T(8,128)S(1)}, f32[256,256]{1,0:T(8,128)}, u32[]{:S(2)}) %copy-start.2) | copy-done | bytes 262168
  3.9 0.0 copy-start.3
  3.9 0.9 %copy-done.3 = f32[32,1024]{1,0:T(8,128)S(1)} copy-done((f32[32,1024]{1,0:T(8,128)S(1)}, f32[32,1024]{1,0:T(8,128)}, u32[]{:S(2)}) %copy-start.3) | copy-done | bytes 131096
  4.8 0.0 copy-start.4
  4.8 0.9 %copy-done.4 = f32[32,1024]{1,0:T(8,128)S(1)} copy-done((f32[32,1024]{1,0:T(8,128)S(1)}, f32[32,1024]{1,0:T(8,128)}, u32[]{:S(2)}) %copy-start.4) | copy-done | bytes 131096
  5.7 21.7 %shard_map.91 = f32[32,1024]{1,0:T(8,128)S(1)} custom-call(s32[8,3]{1,0:T(8,128)S(1)} %copy.10.links, s32[4,3]{1,0:T(4,128)S(1)} %copy-done.6, f32[32,1024]{1,0:T(8,128)S(1)} %copy-done.3, f32[32,1024]{1,0:T(8,128)S(1)} %copy-done.4, bf16[8,3,128,128]{3,2,1,0:T(8,128)(2,1)S(1)} %copy-done, s32[8,128]{1,0:T(8,128)S(1)} %bitcast.2, ...), custom_call_target="tpu_custom_call" | custom-call | tf_op jit(solution)/shard_map/pallas_call | solution.py:391
  27.5 0.7 %copy.12 = f32[32,1024]{1,0:T(8,128)} copy(f32[32,1024]{1,0:T(8,128)S(1)} %shard_map.91) | data formatting | bytes 262144
Async XLA Ops:
  0.0 0.8 %copy-start.7 = (s32[512]{0:T(512)S(1)}, s32[512]{0:T(512)}, u32[]{:S(2)}) copy-start(s32[512]{0:T(512)} %param.16) | copy-start | bytes 6148
  0.0 0.8 %copy-start.5 = (s32[1024]{0:T(1024)S(1)}, s32[1024]{0:T(1024)}, u32[]{:S(2)}) copy-start(s32[1024]{0:T(1024)} %param.13) | copy-start | bytes 12292
  0.0 0.8 %copy-start.6 = (s32[4,3]{1,0:T(4,128)S(1)}, s32[4,3]{1,0:T(4,128)}, u32[]{:S(2)}) copy-start(s32[4,3]{1,0:T(4,128)} %mid_links.1) | copy-start | bytes 148
  0.8 1.1 %copy-start = (bf16[8,3,128,128]{3,2,1,0:T(8,128)(2,1)S(1)}, bf16[8,3,128,128]{3,2,1,0:T(8,128)(2,1)}, u32[]{:S(2)}) copy-start(bf16[8,3,128,128]{3,2,1,0:T(8,128)(2,1)} %t_any.1) | copy-start | bytes 2359300
  1.9 1.0 %copy-start.1 = (bf16[4,3,128,128]{3,2,1,0:T(8,128)(2,1)S(1)}, bf16[4,3,128,128]{3,2,1,0:T(8,128)(2,1)}, u32[]{:S(2)}) copy-start(bf16[4,3,128,128]{3,2,1,0:T(8,128)(2,1)} %mt_any.1) | copy-start | bytes 1179652
  2.9 0.9 %copy-start.2 = (f32[256,256]{1,0:T(8,128)S(1)}, f32[256,256]{1,0:T(8,128)}, u32[]{:S(2)}) copy-start(f32[256,256]{1,0:T(8,128)} %li_any.1) | copy-start | bytes 786436
  3.9 0.9 %copy-start.3 = (f32[32,1024]{1,0:T(8,128)S(1)}, f32[32,1024]{1,0:T(8,128)}, u32[]{:S(2)}) copy-start(f32[32,1024]{1,0:T(8,128)} %b_any.1) | copy-start | bytes 393220
  4.8 0.9 %copy-start.4 = (f32[32,1024]{1,0:T(8,128)S(1)}, f32[32,1024]{1,0:T(8,128)}, u32[]{:S(2)}) copy-start(f32[32,1024]{1,0:T(8,128)} %u_any.1) | copy-start | bytes 393220

commit v2 on v1

--- a/solution.py
+++ b/solution.py
@@ -38,8 +38,9 @@
     return total
 
 
-def one_hot_t(groups, base, rows):
-    ids = lax.broadcasted_iota(jnp.int32, (rows, groups.shape[1]), 0) + base
+def one_hot_t(groups, base, rows, period):
+    ids = lax.broadcasted_iota(jnp.int32, (rows, groups.shape[1]), 0)
+    ids = lax.rem(ids, period) + base
     return jnp.where(ids == groups, 1.0, 0.0).astype(BF16)
 
 
@@ -79,6 +80,7 @@
     ends_f,
     grp_h,
     slabs,
+    own_pick,
     pt,
     ct,
     e_hi,
@@ -94,7 +96,8 @@
     blocks, tile = t_v.shape[0], t_v.shape[2]
     mid_blocks = mt_v.shape[0]
     last = li_v.shape[0]
-    per = n // mid_blocks
+    window = mid_blocks * tile // n
+    assert 2 * window == tile
     me = lax.axis_index("rows") * sub + lax.axis_index("sub")
     has_left = me > 0
     has_right = me < n - 1
@@ -221,16 +224,13 @@
         return [dot_nt(xb[g + 1], t_v[g, 0]) for g in range(blocks)]
 
     def rest(xb, g):
-        picked = jnp.concatenate([xb[links[g, 1]], xb[links[g, 2]]], axis=1)
+        picked = jnp.concatenate([xb[links[1, g]], xb[links[2, g]]], axis=1)
         return dot_nt(picked, jnp.concatenate([t_v[g, 1], t_v[g, 2]], axis=1))
 
     loads[2].wait()
     loads[3].wait()
     acc = own(xb0)
     scale = [scale_of(t_v[g, 0]) for g in range(blocks)]
-    base = lax.div(me, per) * tile
-    for g in range(blocks):
-        pt[:, cells[g]] = one_hot_t(grp_v[g : g + 1], base, tile)
 
     recv(0)
     for g in order:
@@ -241,16 +241,8 @@
             send(1)
     acc = own(xb1)
 
-    for i in (4, 5, 6):
-        loads[i].wait()
-    flipped = li_v[...].T
-    flipped_hi = flipped.astype(BF16)
-    flipped_lo = (flipped - flipped_hi.astype(F32)).astype(BF16)
-    for m in range(mid_blocks):
-        hot = one_hot_t(mg_v[m : m + 1], 0, last)
-        ct[m] = hot
-        e_hi[m] = dot_nn(flipped_hi, hot).astype(BF16)
-        e_lo[m] = dot_nn(flipped_lo, hot).astype(BF16)
+    for g in range(blocks):
+        own_pick[:, cells[g]] = one_hot_t(grp_v[g : g + 1], me * window, tile, window)
 
     recv(1)
     for g in order:
@@ -263,7 +255,6 @@
             ends_f[1] = new
             send(2)
     acc = own(xb2)
-    mid_scale = [scale_of(mt_v[m, 0]) for m in range(mid_blocks)]
 
     recv(2)
     xb2[0] = halo_f[0].astype(BF16)
@@ -271,7 +262,11 @@
     resid = jnp.concatenate(
         [pieces(b_v[:, cells[g]] - (acc[g] + rest(xb2, g)), 3) for g in range(blocks)], axis=1
     )
-    slabs[me] = unstack(dot_nt(resid, pt[...]), 3)
+    sums = unstack(dot_nt(resid, own_pick[...]), 3)
+    half = sums.shape[0] // 2
+    low = lax.broadcasted_iota(jnp.int32, (half, tile), 1) < window
+    odd = lax.rem(me, 2) == 1
+    slabs[me] = jnp.where(jnp.logical_xor(low, odd), sums[:half], sums[half:])
     gathers = []
     for off in range(n - 1, 0, -1):
         copy = pltpu.make_async_remote_copy(
@@ -284,18 +279,32 @@
         )
         copy.start()
         gathers.append(copy)
+
+    for i in (4, 5, 6):
+        loads[i].wait()
+    flipped = li_v[...].T
+    flipped_hi = flipped.astype(BF16)
+    flipped_lo = (flipped - flipped_hi.astype(F32)).astype(BF16)
+    for m in range(mid_blocks):
+        hot = one_hot_t(mg_v[m : m + 1], 0, last, last)
+        ct[m] = hot
+        e_hi[m] = dot_nn(flipped_hi, hot).astype(BF16)
+        e_lo[m] = dot_nn(flipped_lo, hot).astype(BF16)
+    mid_scale = [scale_of(mt_v[m, 0]) for m in range(mid_blocks)]
+    for g in range(blocks):
+        pt[:, cells[g]] = one_hot_t(grp_v[g : g + 1], lax.div(me, 2) * tile, tile, tile)
     recv(4)
-    hot_left = one_hot_t(grp_h[0, blocks - 1 : blocks], lax.div(left, per) * tile, tile)
-    hot_right = one_hot_t(grp_h[1, 0:1], lax.div(right, per) * tile, tile)
+    hot_left = one_hot_t(grp_h[0, blocks - 1 : blocks], lax.div(left, 2) * tile, tile, tile)
+    hot_right = one_hot_t(grp_h[1, 0:1], lax.div(right, 2) * tile, tile, tile)
     for copy in gathers:
         copy.wait_recv()
 
     side = []
     for m in range(mid_blocks):
-        total = slabs[m * per]
-        for i in range(1, per):
-            total = total + slabs[m * per + i]
-        side.append(total)
+        even, other = slabs[2 * m], slabs[2 * m + 1]
+        top = jnp.where(low, even, other)
+        bottom = pltpu.roll(jnp.where(low, other, even), window, 1)
+        side.append(jnp.concatenate([top, bottom], axis=0))
 
     def mid_apply(values):
         for m in range(mid_blocks):
@@ -333,7 +342,7 @@
         mid_v[m] = mid[m]
 
     def lift(device, hot):
-        return unstack(dot_nn(pieces(mid_v[lax.div(device, per)], 3), hot), 3)
+        return unstack(dot_nn(pieces(mid_v[lax.div(device, 2)], 3), hot), 3)
 
     add = lift(me, pt[...])
     before = halo_f[0] + lift(left, hot_left)
@@ -382,7 +391,7 @@
     mid_blocks = mid_tiles.shape[0]
     rows = right_side.shape[0]
     last = last_inverse.shape[0]
-    anywhere = pl.BlockSpec(memory_space=pl.ANY)
+    anywhere = pl.BlockSpec(memory_space=pltpu.HBM)
     scalars = pl.BlockSpec(memory_space=pltpu.SMEM)
     groups = fine_groups.reshape(blocks, tile)
     mid_groups = mid_groups.reshape(mid_blocks, tile)
@@ -399,7 +408,8 @@
             pltpu.VMEM((2, rows, tile), F32),
             pltpu.VMEM((2, rows, tile), F32),
             pltpu.VMEM((2, blocks, tile), jnp.int32),
-            pltpu.VMEM((n, rows, tile), F32),
+            pltpu.VMEM((n, rows // 2, tile), F32),
+            pltpu.VMEM((tile, blocks * tile), BF16),
             pltpu.VMEM((tile, blocks * tile), BF16),
             pltpu.VMEM((mid_blocks, last, tile), BF16),
             pltpu.VMEM((mid_blocks, last, tile), BF16),
@@ -413,9 +423,9 @@
             pltpu.SemaphoreType.DMA((n - 1,)),
         ],
         compiler_params=pltpu.CompilerParams(
-            collective_id=0, has_side_effects=True, vmem_limit_bytes=48 * 1024 * 1024
+            collective_id=0, has_side_effects=True, vmem_limit_bytes=60 * 1024 * 1024
         ),
-    )(fine_links, mid_links, *large)
+    )(fine_links.T, mid_links, *large)
 
 
 def solution(mesh):

time: 28.4 us -> 23 us (0.81)
  local copies, waits for them, and re-layouts: 6.34 us -> 1.57 us
  Pallas kernels: 21.7 us -> 21.2 us
    unnamed x18 -> x1, local copies, waits for them, and re-layouts: 6.34 us -> 1.57 us
    pallas_call x1, Pallas kernels: 21.7 us -> 21.2 us  [shards(): pl.pallas_call(functools.partial(kernel, n, sub), out_shape=jax.ShapeDtyp...]
where the time goes in v2:
time: 23 us; the launch traced here: 22.8 us
  Pallas kernels  21.2 us (92%)
  local copies, waits for them, and re-layouts  1.57 us (7%)
    pallas_call x1, Pallas kernels, shards(): pl.pallas_call(functools.partial(kernel, n, sub), out_shape=jax.ShapeDtyp...  21.2 us
    unnamed x1, local copies, waits for them, and re-layouts  1.57 us

profile of v2, /device:TPU:1, one launch (start us, length us, event | category | flops | bytes accessed | tf_op | source)
XLA Modules:
  0.0 22.8 jit_solution(18162415859189984526)
XLA Ops:
  0.0 21.2 %shard_map.91 = f32[32,1024]{1,0:T(8,128)} custom-call(s32[3,8]{1,0:T(4,128)} %bitcast.4, s32[4,3]{1,0:T(4,128)} %mid_links.1, f32[32,1024]{1,0:T(8,128)} %b_any.1, f32[32,1024]{1,0:T(8,128)} %u_any.1, bf16[8,3,128,128]{3,2,1,0:T(8,128)(2,1)} %t_any.1, s32[8,128]{1,0:T(8,128)} %bitcast.3, bf16[4,3,128,128]{3,2,1,0:T(8,128)(2,1)} %mt_any.1, ...), custom_call_target="tpu_custom_call" | custom-call | tf_op jit(solution)/shard_map/pallas_call | solution.py:400
  21.2 1.6 %copy.11 = f32[32,1024]{1,0:T(8,128)} copy(f32[32,1024]{1,0:T(8,128)} %shard_map.91) | data formatting | bytes 262144

commit v3 on v2

--- a/solution.py
+++ b/solution.py
@@ -76,9 +76,21 @@
     xb2,
     xb3,
     xb4,
-    halo_f,
-    ends_f,
-    grp_h,
+    meta_v,
+    meta_h,
+    meta_f,
+    tiles_h,
+    b_h,
+    u1_e,
+    u1_h,
+    pick1,
+    pick1_h,
+    far1_h,
+    u2,
+    u2_h,
+    pick2,
+    pick2_h,
+    far2_h,
     slabs,
     own_pick,
     pt,
@@ -128,86 +140,94 @@
             barrier, inc=1, device_id=place(lax.rem(me + off, n)), device_id_type=MESH
         )
 
-    left = jnp.maximum(me - 1, 0)
-    right = jnp.minimum(me + 1, n - 1)
-
-    def to_left(i, src, dst):
-        return pltpu.make_async_remote_copy(
-            src_ref=src,
-            dst_ref=dst,
-            send_sem=halo_send.at[i, 0],
-            recv_sem=halo_recv.at[i, 1],
-            device_id=place(left),
-            device_id_type=MESH,
-        )
-
-    def to_right(i, src, dst):
-        return pltpu.make_async_remote_copy(
-            src_ref=src,
-            dst_ref=dst,
-            send_sem=halo_send.at[i, 1],
-            recv_sem=halo_recv.at[i, 0],
-            device_id=place(right),
-            device_id_type=MESH,
-        )
-
-    def pair(i, first, final, before, after):
-        return to_left(i, first, after), to_right(i, final, before)
-
-    def ends(i, xb):
-        return pair(i, xb.at[1], xb.at[blocks], xb.at[0], xb.at[blocks + 1])
-
+    left, left2 = jnp.maximum(me - 1, 0), jnp.maximum(me - 2, 0)
+    right, right2 = jnp.minimum(me + 1, n - 1), jnp.minimum(me + 2, n - 1)
+
+    def pair(i, first, final, arrived, far=False):
+        def copy(src, side, device):
+            return pltpu.make_async_remote_copy(
+                src_ref=src,
+                dst_ref=arrived[1 - side],
+                send_sem=halo_send.at[i, side],
+                recv_sem=halo_recv.at[i, 1 - side],
+                device_id=place(device),
+                device_id_type=MESH,
+            )
+
+        to_left = copy(first, 0, left2 if far else left)
+        to_right = copy(final, 1, right2 if far else right)
+        return to_left, to_right, (me > 1 if far else has_left), (me < n - 2 if far else has_right)
+
+    def sides(ref):
+        return ref.at[0], ref.at[1]
+
+    edge = slice(0, tile), slice((blocks - 1) * tile, blocks * tile)
     swaps = [
-        ends(0, xb0),
-        ends(1, xb1),
-        pair(2, ends_f.at[0], ends_f.at[1], halo_f.at[0], halo_f.at[1]),
-        ends(3, xb4),
-        pair(4, grp_v, grp_v, grp_h.at[0], grp_h.at[1]),
+        pair(0, xb0.at[1], xb0.at[blocks], (xb0.at[0], xb0.at[blocks + 1])),
+        pair(1, meta_v, meta_v, sides(meta_h)),
+        pair(2, t_v.at[0], t_v.at[blocks - 1], sides(tiles_h)),
+        pair(3, b_v.at[:, edge[0]], b_v.at[:, edge[1]], sides(b_h)),
+        pair(4, u1_e.at[0], u1_e.at[1], sides(u1_h)),
+        pair(5, pick1.at[0], pick1.at[1], sides(pick1_h)),
+        pair(6, xb1.at[1], xb1.at[blocks], sides(far1_h), far=True),
+        pair(7, meta_v, meta_v, sides(meta_f), far=True),
+        pair(8, pick2.at[0], pick2.at[1], sides(pick2_h)),
+        pair(9, u2.at[0], u2.at[blocks - 1], sides(far2_h), far=True),
     ]
 
     def send(i):
-        @pl.when(has_left)
-        def _():
-            swaps[i][0].start()
-
-        @pl.when(has_right)
-        def _():
-            swaps[i][1].start()
+        to_left, to_right, some_left, some_right = swaps[i]
+
+        @pl.when(some_left)
+        def _():
+            to_left.start()
+
+        @pl.when(some_right)
+        def _():
+            to_right.start()
 
     def recv(i):
-        @pl.when(has_left)
-        def _():
-            swaps[i][1].wait_recv()
-
-        @pl.when(has_right)
-        def _():
-            swaps[i][0].wait_recv()
+        to_left, to_right, some_left, some_right = swaps[i]
+
+        @pl.when(some_left)
+        def _():
+            to_right.wait_recv()
+
+        @pl.when(some_right)
+        def _():
+            to_left.wait_recv()
 
     def sent(i):
-        @pl.when(has_left)
-        def _():
-            swaps[i][0].wait_send()
-
-        @pl.when(has_right)
-        def _():
-            swaps[i][1].wait_send()
-
-    zero_b = jnp.zeros(xb0.shape[1:], BF16)
-    zero_f = jnp.zeros(halo_f.shape[1:], F32)
-
-    @pl.when(me == 0)
-    def _():
-        for xb in (xb0, xb1, xb4):
-            xb[0] = zero_b
-        halo_f[0] = zero_f
-        grp_h[0] = jnp.zeros(grp_h.shape[1:], jnp.int32)
-
-    @pl.when(me == n - 1)
-    def _():
-        for xb in (xb0, xb1, xb4):
-            xb[blocks + 1] = zero_b
-        halo_f[1] = zero_f
-        grp_h[1] = jnp.zeros(grp_h.shape[1:], jnp.int32)
+        to_left, to_right, some_left, some_right = swaps[i]
+
+        @pl.when(some_left)
+        def _():
+            to_left.wait_send()
+
+        @pl.when(some_right)
+        def _():
+            to_right.wait_send()
+
+    def clear(ref, i):
+        ref[i] = jnp.zeros(ref.shape[1:], ref.dtype)
+
+    for i in (0, blocks + 1):
+        clear(xb1, i)
+    for side, near_edge, far_edge in (
+        (0, me == 0, me <= 1),
+        (1, me == n - 1, me >= n - 2),
+    ):
+
+        @pl.when(near_edge)
+        def _():
+            clear(xb0, side * (blocks + 1))
+            for ref in (meta_h, tiles_h, b_h, u1_h, pick1_h, pick2_h):
+                clear(ref, side)
+
+        @pl.when(far_edge)
+        def _():
+            for ref in (meta_f, far1_h, far2_h):
+                clear(ref, side)
 
     order = [0, blocks - 1] + list(range(1, blocks - 1))
     cells = [slice(g * tile, (g + 1) * tile) for g in range(blocks)]
@@ -218,7 +238,15 @@
     loads[1].wait()
     pl.semaphore_wait(barrier, n - 1)
     send(0)
-    send(4)
+    outer = links[2, 0], links[1, blocks - 1]
+    inner = [jnp.clip(link - 1, 0, blocks - 1) for link in outer]
+    meta_v[...] = jnp.zeros(meta_v.shape, jnp.int32)
+    meta_v[0:blocks] = grp_v[...]
+    for side in (0, 1):
+        meta_v[blocks + side : blocks + side + 1] = jnp.full((1, tile), outer[side], jnp.int32)
+        meta_v[blocks + 2 + side : blocks + 3 + side] = grp_v[pl.ds(inner[side], 1)]
+    send(1)
+    send(7)
 
     def own(xb):
         return [dot_nt(xb[g + 1], t_v[g, 0]) for g in range(blocks)]
@@ -228,7 +256,9 @@
         return dot_nt(picked, jnp.concatenate([t_v[g, 1], t_v[g, 2]], axis=1))
 
     loads[2].wait()
+    send(2)
     loads[3].wait()
+    send(3)
     acc = own(xb0)
     scale = [scale_of(t_v[g, 0]) for g in range(blocks)]
 
@@ -237,28 +267,53 @@
         new = u_v[:, cells[g]] + (b_v[:, cells[g]] - (acc[g] + rest(xb0, g))) * scale[g]
         u_v[:, cells[g]] = new
         xb1[g + 1] = new.astype(BF16)
+        if g == 0:
+            u1_e[0] = new
         if g == blocks - 1:
-            send(1)
+            u1_e[1] = new
+            send(6)
+            send(4)
+    for side in (0, 1):
+        pick1[side] = xb1[inner[side] + 1]
+    send(5)
     acc = own(xb1)
 
     for g in range(blocks):
         own_pick[:, cells[g]] = one_hot_t(grp_v[g : g + 1], me * window, tile, window)
 
-    recv(1)
+    def select(side, own, far, near):
+        link = meta_h[side, blocks + 1 - side : blocks + 2 - side]
+        mine, beyond = (blocks + 1, 0) if side == 0 else (0, blocks + 1)
+        return jnp.where(link == mine, own, jnp.where(link == beyond, far, near))
+
+    def follow(side, xb, field, far, near):
+        end, own = xb[side * (blocks + 1)], xb[1 if side == 0 else blocks]
+        other = select(side, own.astype(F32), far, near).astype(BF16)
+        parts = [end, other, own] if side == 0 else [end, own, other]
+        product = dot_nt(
+            jnp.concatenate(parts, axis=1),
+            jnp.concatenate([tiles_h[side, k] for k in range(3)], axis=1),
+        )
+        new = field + (b_h[side] - product) * scale_of(tiles_h[side, 0])
+        return jnp.where(has_right if side else has_left, new, 0.0)
+
+    for i in (1, 2, 3, 4, 5, 6):
+        recv(i)
+    for side in (0, 1):
+        xb1[side * (blocks + 1)] = u1_h[side].astype(BF16)
+    for side in (0, 1):
+        new = follow(
+            side, xb1, u1_h[side], far1_h[side].astype(F32), pick1_h[side].astype(F32)
+        )
+        u2_h[side] = new
+        xb2[side * (blocks + 1)] = new.astype(BF16)
     for g in order:
         new = u_v[:, cells[g]] + (b_v[:, cells[g]] - (acc[g] + rest(xb1, g))) * scale[g]
         u_v[:, cells[g]] = new
+        u2[g] = new
         xb2[g + 1] = new.astype(BF16)
-        if g == 0:
-            ends_f[0] = new
-        if g == blocks - 1:
-            ends_f[1] = new
-            send(2)
     acc = own(xb2)
 
-    recv(2)
-    xb2[0] = halo_f[0].astype(BF16)
-    xb2[blocks + 1] = halo_f[1].astype(BF16)
     resid = jnp.concatenate(
         [pieces(b_v[:, cells[g]] - (acc[g] + rest(xb2, g)), 3) for g in range(blocks)], axis=1
     )
@@ -279,6 +334,10 @@
         )
         copy.start()
         gathers.append(copy)
+    for side in (0, 1):
+        pick2[side] = u2[inner[side]]
+    send(8)
+    send(9)
 
     for i in (4, 5, 6):
         loads[i].wait()
@@ -293,9 +352,20 @@
     mid_scale = [scale_of(mt_v[m, 0]) for m in range(mid_blocks)]
     for g in range(blocks):
         pt[:, cells[g]] = one_hot_t(grp_v[g : g + 1], lax.div(me, 2) * tile, tile, tile)
-    recv(4)
-    hot_left = one_hot_t(grp_h[0, blocks - 1 : blocks], lax.div(left, 2) * tile, tile, tile)
-    hot_right = one_hot_t(grp_h[1, 0:1], lax.div(right, 2) * tile, tile, tile)
+    recv(7)
+
+    def hot(meta, device):
+        return one_hot_t(meta, lax.div(device, 2) * tile, tile, tile)
+
+    beside = ((left, left2, blocks - 1), (right, right2, 0))
+    hots = [
+        (
+            hot(meta_h[side, row : row + 1], near),
+            hot(meta_h[side, blocks + 3 - side : blocks + 4 - side], near),
+            hot(meta_f[side, row : row + 1], far),
+        )
+        for side, (near, far, row) in enumerate(beside)
+    ]
     for copy in gathers:
         copy.wait_recv()
 
@@ -345,25 +415,31 @@
         return unstack(dot_nn(pieces(mid_v[lax.div(device, 2)], 3), hot), 3)
 
     add = lift(me, pt[...])
-    before = halo_f[0] + lift(left, hot_left)
-    after = halo_f[1] + lift(right, hot_right)
-    xb3[0] = jnp.where(has_left, before, 0.0).astype(BF16)
-    xb3[blocks + 1] = jnp.where(has_right, after, 0.0).astype(BF16)
+    recv(8)
+    recv(9)
+    u3_h = []
+    for side, (near, far, _) in enumerate(beside):
+        end = u2_h[side] + lift(near, hots[side][0])
+        end = jnp.where(has_right if side else has_left, end, 0.0)
+        xb3[side * (blocks + 1)] = end.astype(BF16)
+        picked = pick2_h[side] + lift(near, hots[side][1])
+        beyond = far2_h[side] + lift(far, hots[side][2])
+        beyond = jnp.where(me < n - 2 if side else me > 1, beyond, 0.0)
+        u3_h.append((end, beyond, picked))
     for g in range(blocks):
         new = u_v[:, cells[g]] + add[:, cells[g]]
         u_v[:, cells[g]] = new
         xb3[g + 1] = new.astype(BF16)
 
     acc = own(xb3)
+    for side in (0, 1):
+        xb4[side * (blocks + 1)] = follow(side, xb3, *u3_h[side]).astype(BF16)
     for g in order:
         new = u_v[:, cells[g]] + (b_v[:, cells[g]] - (acc[g] + rest(xb3, g))) * scale[g]
         u_v[:, cells[g]] = new
         xb4[g + 1] = new.astype(BF16)
-        if g == blocks - 1:
-            send(3)
     acc = own(xb4)
 
-    recv(3)
     for g in range(blocks):
         out_ref[:, cells[g]] = (
             u_v[:, cells[g]] + (b_v[:, cells[g]] - (acc[g] + rest(xb4, g))) * scale[g]
@@ -405,9 +481,21 @@
         scratch_shapes=[pltpu.VMEM(x.shape, x.dtype) for x in large]
         + [held] * 5
         + [
-            pltpu.VMEM((2, rows, tile), F32),
-            pltpu.VMEM((2, rows, tile), F32),
-            pltpu.VMEM((2, blocks, tile), jnp.int32),
+            pltpu.VMEM((blocks + 8, tile), jnp.int32),
+            pltpu.VMEM((2, blocks + 8, tile), jnp.int32),
+            pltpu.VMEM((2, blocks + 8, tile), jnp.int32),
+            pltpu.VMEM((2,) + fine_tiles.shape[1:], BF16),
+            pltpu.VMEM((2, rows, tile), F32),
+            pltpu.VMEM((2, rows, tile), F32),
+            pltpu.VMEM((2, rows, tile), F32),
+            pltpu.VMEM((2, rows, tile), BF16),
+            pltpu.VMEM((2, rows, tile), BF16),
+            pltpu.VMEM((2, rows, tile), BF16),
+            pltpu.VMEM((blocks, rows, tile), F32),
+            pltpu.VMEM((2, rows, tile), F32),
+            pltpu.VMEM((2, rows, tile), F32),
+            pltpu.VMEM((2, rows, tile), F32),
+            pltpu.VMEM((2, rows, tile), F32),
             pltpu.VMEM((n, rows // 2, tile), F32),
             pltpu.VMEM((tile, blocks * tile), BF16),
             pltpu.VMEM((tile, blocks * tile), BF16),
@@ -417,13 +505,13 @@
             pltpu.VMEM((mid_blocks, rows, tile), BF16),
             pltpu.VMEM((mid_blocks, rows, tile), F32),
             pltpu.SemaphoreType.DMA((len(large),)),
-            pltpu.SemaphoreType.DMA((5, 2)),
-            pltpu.SemaphoreType.DMA((5, 2)),
+            pltpu.SemaphoreType.DMA((10, 2)),
+            pltpu.SemaphoreType.DMA((10, 2)),
             pltpu.SemaphoreType.DMA((n - 1,)),
             pltpu.SemaphoreType.DMA((n - 1,)),
         ],
         compiler_params=pltpu.CompilerParams(
-            collective_id=0, has_side_effects=True, vmem_limit_bytes=60 * 1024 * 1024
+            collective_id=0, has_side_effects=True, vmem_limit_bytes=56308531
         ),
     )(fine_links.T, mid_links, *large)
 

time: 23 us -> 22.1 us (0.961)
  the two profiles are of different devices: /device:TPU:1 before, /device:TPU:0 now
where the time goes in v3:
time: 22.1 us; the launch traced here: 21.9 us
  Pallas kernels  18.5 us (84%)
  local copies, waits for them, and re-layouts  3.39 us (15%)
    pallas_call x1, Pallas kernels, shards(): pl.pallas_call(functools.partial(kernel, n, sub), out_shape=jax.ShapeDtyp...  18.5 us
    unnamed x9, local copies, waits for them, and re-layouts  3.39 us

profile of v3, /device:TPU:0, one launch (start us, length us, event | category | flops | bytes accessed | tf_op | source)
XLA Modules:
  0.0 21.9 jit_solution(1538963734822943835)
XLA Ops:
  0.0 0.0 copy-start
  0.0 0.7 %copy-done = s32[1024]{0:T(1024)S(1)} copy-done((s32[1024]{0:T(1024)S(1)}, s32[1024]{0:T(1024)}, u32[]{:S(2)}) %copy-start) | copy-done | bytes 4120
  0.7 0.0 copy-start.1
  0.7 0.7 %copy-done.1 = s32[8,3]{0,1:T(4,128)S(1)} copy-done((s32[8,3]{0,1:T(4,128)S(1)}, s32[8,3]{0,1:T(4,128)}, u32[]{:S(2)}) %copy-start.1) | copy-done | bytes 120
  1.4 0.0 copy-start.2
  1.4 0.7 %copy-done.2 = s32[4,3]{1,0:T(4,128)S(1)} copy-done((s32[4,3]{1,0:T(4,128)S(1)}, s32[4,3]{1,0:T(4,128)}, u32[]{:S(2)}) %copy-start.2) | copy-done | bytes 72
  2.1 0.0 copy-start.3
  2.1 0.7 %copy-done.3 = s32[512]{0:T(512)S(1)} copy-done((s32[512]{0:T(512)S(1)}, s32[512]{0:T(512)}, u32[]{:S(2)}) %copy-start.3) | copy-done | bytes 2072
  2.7 18.5 %shard_map.91 = f32[32,1024]{1,0:T(8,128)S(1)} custom-call(s32[3,8]{1,0:T(4,128)S(1)} %bitcast.4, s32[4,3]{1,0:T(4,128)S(1)} %copy-done.2, f32[32,1024]{1,0:T(8,128)} %b_any.1, f32[32,1024]{1,0:T(8,128)} %u_any.1, bf16[8,3,128,128]{3,2,1,0:T(8,128)(2,1)} %t_any.1, s32[8,128]{1,0:T(8,128)S(1)} %bitcast.3, bf16[4,3,128,128]{3,2,1,0:T(8,128)(2,1)} %mt_any.1, ...), custom_call_target="tpu_custom_call" | custom-call | tf_op jit(solution)/shard_map/pallas_call | solution.py:476
  21.2 0.7 %copy.11 = f32[32,1024]{1,0:T(8,128)} copy(f32[32,1024]{1,0:T(8,128)S(1)} %shard_map.91) | data formatting | bytes 262144
Async XLA Ops:
  0.0 0.7 %copy-start = (s32[1024]{0:T(1024)S(1)}, s32[1024]{0:T(1024)}, u32[]{:S(2)}) copy-start(s32[1024]{0:T(1024)} %param.13) | copy-start | bytes 12292
  0.7 0.7 %copy-start.1 = (s32[8,3]{0,1:T(4,128)S(1)}, s32[8,3]{0,1:T(4,128)}, u32[]{:S(2)}) copy-start(s32[8,3]{0,1:T(4,128)} %param.12) | copy-start | bytes 292
  1.4 0.7 %copy-start.2 = (s32[4,3]{1,0:T(4,128)S(1)}, s32[4,3]{1,0:T(4,128)}, u32[]{:S(2)}) copy-start(s32[4,3]{1,0:T(4,128)} %mid_links.1) | copy-start | bytes 148
  2.1 0.7 %copy-start.3 = (s32[512]{0:T(512)S(1)}, s32[512]{0:T(512)}, u32[]{:S(2)}) copy-start(s32[512]{0:T(512)} %param.16) | copy-start | bytes 6148

commit v4 on v3

--- a/solution.py
+++ b/solution.py
@@ -104,6 +104,7 @@
     halo_recv,
     all_send,
     all_recv,
+    round_sem,
 ):
     blocks, tile = t_v.shape[0], t_v.shape[2]
     mid_blocks = mt_v.shape[0]
@@ -134,11 +135,25 @@
     for load in loads:
         load.start()
 
+    def greet(sem, distance):
+        for there in (me - distance, me + distance):
+
+            @pl.when(jnp.logical_and(there >= 0, there < n))
+            def _():
+                pl.semaphore_signal(sem, inc=1, device_id=place(there), device_id_type=MESH)
+
+    def greeted(sem, *distances):
+        count = jnp.int32(0)
+        for distance in distances:
+            count = count + jnp.where(me >= distance, 1, 0) + jnp.where(me + distance < n, 1, 0)
+        pl.semaphore_wait(sem, count)
+
     barrier = pltpu.get_barrier_semaphore()
-    for off in range(1, n):
-        pl.semaphore_signal(
-            barrier, inc=1, device_id=place(lax.rem(me + off, n)), device_id_type=MESH
-        )
+    for distance in (1, 2):
+        greet(barrier, distance)
+    reaches = [2]
+    while 2 * reaches[-1] < n - 1:
+        reaches.append(2 * reaches[-1])
 
     left, left2 = jnp.maximum(me - 1, 0), jnp.maximum(me - 2, 0)
     right, right2 = jnp.minimum(me + 1, n - 1), jnp.minimum(me + 2, n - 1)
@@ -236,9 +251,10 @@
     for g in order:
         xb0[g + 1] = u_v[:, cells[g]].astype(BF16)
     loads[1].wait()
-    pl.semaphore_wait(barrier, n - 1)
+    greeted(barrier, 1, 2)
     send(0)
-    outer = links[2, 0], links[1, blocks - 1]
+    greet(round_sem.at[0], reaches[0])
+    outer = links[0, 2], links[blocks - 1, 1]
     inner = [jnp.clip(link - 1, 0, blocks - 1) for link in outer]
     meta_v[...] = jnp.zeros(meta_v.shape, jnp.int32)
     meta_v[0:blocks] = grp_v[...]
@@ -252,7 +268,7 @@
         return [dot_nt(xb[g + 1], t_v[g, 0]) for g in range(blocks)]
 
     def rest(xb, g):
-        picked = jnp.concatenate([xb[links[1, g]], xb[links[2, g]]], axis=1)
+        picked = jnp.concatenate([xb[links[g, 1]], xb[links[g, 2]]], axis=1)
         return dot_nt(picked, jnp.concatenate([t_v[g, 1], t_v[g, 2]], axis=1))
 
     loads[2].wait()
@@ -276,6 +292,9 @@
     for side in (0, 1):
         pick1[side] = xb1[inner[side] + 1]
     send(5)
+    greeted(round_sem.at[0], reaches[0])
+    if len(reaches) > 1:
+        greet(round_sem.at[1], reaches[1])
     acc = own(xb1)
 
     for g in range(blocks):
@@ -322,6 +341,10 @@
     low = lax.broadcasted_iota(jnp.int32, (half, tile), 1) < window
     odd = lax.rem(me, 2) == 1
     slabs[me] = jnp.where(jnp.logical_xor(low, odd), sums[:half], sums[half:])
+    for i in range(1, len(reaches)):
+        greeted(round_sem.at[i], reaches[i])
+        if i + 1 < len(reaches):
+            greet(round_sem.at[i + 1], reaches[i + 1])
     gathers = []
     for off in range(n - 1, 0, -1):
         copy = pltpu.make_async_remote_copy(
@@ -509,11 +532,12 @@
             pltpu.SemaphoreType.DMA((10, 2)),
             pltpu.SemaphoreType.DMA((n - 1,)),
             pltpu.SemaphoreType.DMA((n - 1,)),
+            pltpu.SemaphoreType.REGULAR((8,)),
         ],
         compiler_params=pltpu.CompilerParams(
             collective_id=0, has_side_effects=True, vmem_limit_bytes=56308531
         ),
-    )(fine_links.T, mid_links, *large)
+    )(fine_links, mid_links, *large)
 
 
 def solution(mesh):

time: 22.1 us -> 19.9 us (0.900)
  local copies, waits for them, and re-layouts: 3.39 us -> 1.47 us
    unnamed x9 -> x8, local copies, waits for them, and re-layouts: 3.39 us -> 1.47 us
where the time goes in v4:
time: 19.9 us; the launch traced here: 19.8 us
  Pallas kernels  18.3 us (92%)
  local copies, waits for them, and re-layouts  1.47 us (7%)
    pallas_call x1, Pallas kernels, shards(): pl.pallas_call(functools.partial(kernel, n, sub), out_shape=jax.ShapeDtyp...  18.3 us
    unnamed x8, local copies, waits for them, and re-layouts  1.47 us

profile of v4, /device:TPU:0, one launch (start us, length us, event | category | flops | bytes accessed | tf_op | source)
XLA Modules:
  0.0 19.8 jit_solution(5043736666378674491)
XLA Ops:
  0.0 0.0 copy-start.2
  0.0 0.0 copy-start
  0.0 0.0 copy-start.1
  0.0 0.8 %copy.10.links = s32[8,3]{1,0:T(8,128)S(1)} copy(s32[8,3]{0,1:T(4,128)} %param.12) | data formatting | bytes 192 | tf_op args[3]
  0.8 0.0 copy-done.2
  0.8 0.0 copy-done
  0.8 0.0 copy-done.1
  0.8 18.3 %shard_map.91 = f32[32,1024]{1,0:T(8,128)S(1)} custom-call(s32[8,3]{1,0:T(8,128)S(1)} %copy.10.links, s32[4,3]{1,0:T(4,128)S(1)} %copy-done.1, f32[32,1024]{1,0:T(8,128)} %b_any.1, f32[32,1024]{1,0:T(8,128)} %u_any.1, bf16[8,3,128,128]{3,2,1,0:T(8,128)(2,1)} %t_any.1, s32[8,128]{1,0:T(8,128)S(1)} %bitcast.2, bf16[4,3,128,128]{3,2,1,0:T(8,128)(2,1)} %mt_any.1, ...), custom_call_target="tpu_custom_call" | custom-call | tf_op jit(solution)/shard_map/pallas_call | solution.py:499
  19.1 0.7 %copy.12 = f32[32,1024]{1,0:T(8,128)} copy(f32[32,1024]{1,0:T(8,128)S(1)} %shard_map.91) | data formatting | bytes 262144
Async XLA Ops:
  0.0 0.8 %copy-start.2 = (s32[512]{0:T(512)S(1)}, s32[512]{0:T(512)}, u32[]{:S(2)}) copy-start(s32[512]{0:T(512)} %param.16) | copy-start | bytes 6148
  0.0 0.8 %copy-start = (s32[1024]{0:T(1024)S(1)}, s32[1024]{0:T(1024)}, u32[]{:S(2)}) copy-start(s32[1024]{0:T(1024)} %param.13) | copy-start | bytes 12292
  0.0 0.8 %copy-start.1 = (s32[4,3]{1,0:T(4,128)S(1)}, s32[4,3]{1,0:T(4,128)}, u32[]{:S(2)}) copy-start(s32[4,3]{1,0:T(4,128)} %mid_links.1) | copy-start | bytes 148

commit v5 on v4

--- a/solution.py
+++ b/solution.py
@@ -54,8 +54,8 @@
 def kernel(
     n,
     sub,
-    links,
-    mid_links,
+    links_any,
+    mid_links_any,
     b_any,
     u_any,
     t_any,
@@ -99,6 +99,8 @@
     e_lo,
     mb,
     mid_v,
+    links,
+    mid_links,
     load_sem,
     halo_send,
     halo_recv,
@@ -129,12 +131,11 @@
                 (mg_any, mg_v),
                 (li_any, li_v),
                 (mt_any, mt_v),
+                (links_any, links),
+                (mid_links_any, mid_links),
             )
         )
     ]
-    for load in loads:
-        load.start()
-
     def greet(sem, distance):
         for there in (me - distance, me + distance):
 
@@ -151,6 +152,8 @@
     barrier = pltpu.get_barrier_semaphore()
     for distance in (1, 2):
         greet(barrier, distance)
+    for load in loads:
+        load.start()
     reaches = [2]
     while 2 * reaches[-1] < n - 1:
         reaches.append(2 * reaches[-1])
@@ -254,6 +257,7 @@
     greeted(barrier, 1, 2)
     send(0)
     greet(round_sem.at[0], reaches[0])
+    loads[7].wait()
     outer = links[0, 2], links[blocks - 1, 1]
     inner = [jnp.clip(link - 1, 0, blocks - 1) for link in outer]
     meta_v[...] = jnp.zeros(meta_v.shape, jnp.int32)
@@ -362,7 +366,7 @@
     send(8)
     send(9)
 
-    for i in (4, 5, 6):
+    for i in (4, 5, 6, 8):
         loads[i].wait()
     flipped = li_v[...].T
     flipped_hi = flipped.astype(BF16)
@@ -491,7 +495,6 @@
     rows = right_side.shape[0]
     last = last_inverse.shape[0]
     anywhere = pl.BlockSpec(memory_space=pltpu.HBM)
-    scalars = pl.BlockSpec(memory_space=pltpu.SMEM)
     groups = fine_groups.reshape(blocks, tile)
     mid_groups = mid_groups.reshape(mid_blocks, tile)
     large = [right_side, start_field, fine_tiles, groups, mid_tiles, mid_groups, last_inverse]
@@ -499,7 +502,7 @@
     return pl.pallas_call(
         functools.partial(kernel, n, sub),
         out_shape=jax.ShapeDtypeStruct(right_side.shape, F32),
-        in_specs=[scalars] * 2 + [anywhere] * len(large),
+        in_specs=[anywhere] * (2 + len(large)),
         out_specs=pl.BlockSpec(memory_space=pltpu.VMEM),
         scratch_shapes=[pltpu.VMEM(x.shape, x.dtype) for x in large]
         + [held] * 5
@@ -527,7 +530,9 @@
             pltpu.VMEM((mid_blocks, last, tile), BF16),
             pltpu.VMEM((mid_blocks, rows, tile), BF16),
             pltpu.VMEM((mid_blocks, rows, tile), F32),
-            pltpu.SemaphoreType.DMA((len(large),)),
+            pltpu.SMEM(fine_links.shape, jnp.int32),
+            pltpu.SMEM(mid_links.shape, jnp.int32),
+            pltpu.SemaphoreType.DMA((2 + len(large),)),
             pltpu.SemaphoreType.DMA((10, 2)),
             pltpu.SemaphoreType.DMA((10, 2)),
             pltpu.SemaphoreType.DMA((n - 1,)),

time: 19.9 us -> 19.4 us (0.975)
  Pallas kernels: 18.3 us -> 17.7 us
    pallas_call x1, Pallas kernels: 18.3 us -> 17.7 us  [shards(): pl.pallas_call(functools.partial(kernel, n, sub), out_shape=jax.ShapeDtyp...]
where the time goes in v5:
time: 19.4 us; the launch traced here: 19.2 us
  Pallas kernels  17.7 us (91%)
  local copies, waits for them, and re-layouts  1.47 us (8%)
    pallas_call x1, Pallas kernels, shards(): pl.pallas_call(functools.partial(kernel, n, sub), out_shape=jax.ShapeDtyp...  17.7 us
    unnamed x8, local copies, waits for them, and re-layouts  1.47 us

profile of v5, /device:TPU:0, one launch (start us, length us, event | category | flops | bytes accessed | tf_op | source)
XLA Modules:
  0.0 19.2 jit_solution(16488189938091233751)
XLA Ops:
  0.0 0.0 copy-start.2
  0.0 0.0 copy-start
  0.0 0.0 copy-start.1
  0.0 0.8 %copy.10.links_any = s32[8,3]{1,0:T(8,128)S(1)} copy(s32[8,3]{0,1:T(4,128)} %param.12) | data formatting | bytes 192 | tf_op args[3]
  0.8 0.0 copy-done.2
  0.8 0.0 copy-done
  0.8 0.0 copy-done.1
  0.8 17.7 %shard_map.91 = f32[32,1024]{1,0:T(8,128)S(1)} custom-call(s32[8,3]{1,0:T(8,128)S(1)} %copy.10.links_any, s32[4,3]{1,0:T(4,128)S(1)} %copy-done.1, f32[32,1024]{1,0:T(8,128)} %b_any.1, f32[32,1024]{1,0:T(8,128)} %u_any.1, bf16[8,3,128,128]{3,2,1,0:T(8,128)(2,1)} %t_any.1, s32[8,128]{1,0:T(8,128)S(1)} %bitcast.2, bf16[4,3,128,128]{3,2,1,0:T(8,128)(2,1)} %mt_any.1, ...), custom_call_target="tpu_custom_call" | custom-call | tf_op jit(solution)/shard_map/pallas_call | solution.py:502
  18.5 0.7 %copy.12 = f32[32,1024]{1,0:T(8,128)} copy(f32[32,1024]{1,0:T(8,128)S(1)} %shard_map.91) | data formatting | bytes 262144
Async XLA Ops:
  0.0 0.8 %copy-start.2 = (s32[512]{0:T(512)S(1)}, s32[512]{0:T(512)}, u32[]{:S(2)}) copy-start(s32[512]{0:T(512)} %param.16) | copy-start | bytes 6148
  0.0 0.8 %copy-start = (s32[1024]{0:T(1024)S(1)}, s32[1024]{0:T(1024)}, u32[]{:S(2)}) copy-start(s32[1024]{0:T(1024)} %param.13) | copy-start | bytes 12292
  0.0 0.8 %copy-start.1 = (s32[4,3]{1,0:T(4,128)S(1)}, s32[4,3]{1,0:T(4,128)}, u32[]{:S(2)}) copy-start(s32[4,3]{1,0:T(4,128)} %mid_links_any.1) | copy-start | bytes 148
